TPU v7x, 128 devices: a whole 4x4x4 slice. The times are simulated.
128 devices in a mesh: row: 16 (over y, x), col: 8 (over z, core).
Axes of the slice: x: 4, y: 4, z: 4, core: 2. Of those that a mesh axis runs over, the one named last changes fastest.
Arguments:
- inputs: bfloat16 [1024, 8192], P('col', 'row'), may hold values from -6 to 6
- out_grad: bfloat16 [1024, 8192], P('col', 'row'), may hold values from -1.5 to 1.5
- gate_pre: bfloat16 [1024, 14336], P('row', 'col'), may hold values from -9 to 9
- up_pre: bfloat16 [1024, 14336], P('row', 'col'), may hold values from -6 to 6
- gate_weight: bfloat16 [8192, 14336], P('row', 'col'), may hold values from -0.0625 to 0.0625
- up_weight: bfloat16 [8192, 14336], P('row', 'col'), may hold values from -0.0625 to 0.0625
- down_weight: bfloat16 [14336, 8192], P('col', 'row'), may hold values from -0.046875 to 0.046875
Outputs:
- input_grad: float32 [1024, 8192], P('col', 'row')
- gate_grad: float32 [8192, 14336], P('row', 'col')
- up_grad: float32 [8192, 14336], P('row', 'col')
- down_grad: float32 [14336, 8192], P('col', 'row')
All inputs are finite; a program needn't handle non-finite values.
Results may differ from a plain program's by a relative error of at most 0.0029.
Values may be sent and summed in bfloat16 or wider, within the bound.
A program may use at most 128 MiB of HBM per device.

v0:
```python
import jax
import jax.numpy as jnp
from jax import lax
from jax.sharding import PartitionSpec as P

LEAD_DIMS = (((0,), (0,)), ((), ()))
LAST_DIMS = (((1,), (1,)), ((), ()))


def body(inputs, out_grad, gate_pre, up_pre, gate_weight, up_weight, down_weight):
    gate_val = gate_pre.astype(jnp.float32)
    up_val = up_pre.astype(jnp.float32)
    gate_sig = jax.nn.sigmoid(gate_val)
    hidden = (gate_val * gate_sig * up_val).astype(jnp.bfloat16)
    grad_full = lax.all_gather(out_grad, "col", axis=0, tiled=True)
    hidden_all = lax.all_gather(hidden, "row", axis=0, tiled=True)
    partial_sum = lax.dot_general(
        grad_full, down_weight, LAST_DIMS, preferred_element_type=jnp.float32
    )
    grad_hidden = lax.psum_scatter(partial_sum, "row", scatter_dimension=0, tiled=True)
    input_full = lax.all_gather(inputs, "col", axis=0, tiled=True)
    grad_gate = (grad_hidden * up_val * gate_sig * (1.0 + gate_val * (1.0 - gate_sig))).astype(
        jnp.bfloat16
    )
    grad_up = (grad_hidden * gate_val * gate_sig).astype(jnp.bfloat16)
    down_grad = lax.dot_general(
        hidden_all, grad_full, LEAD_DIMS, preferred_element_type=jnp.float32
    )
    gate_all = lax.all_gather(grad_gate, "row", axis=0, tiled=True)
    up_all = lax.all_gather(grad_up, "row", axis=0, tiled=True)
    total = lax.dot_general(gate_all, gate_weight, LAST_DIMS, preferred_element_type=jnp.float32)
    input_grad = lax.psum_scatter(
        total + lax.dot_general(up_all, up_weight, LAST_DIMS, preferred_element_type=jnp.float32),
        "col",
        scatter_dimension=0,
        tiled=True,
    )
    gate_grad = lax.dot_general(input_full, gate_all, LEAD_DIMS, preferred_element_type=jnp.float32)
    up_grad = lax.dot_general(input_full, up_all, LEAD_DIMS, preferred_element_type=jnp.float32)
    return (input_grad, gate_grad, up_grad, down_grad)


def solution(mesh):
    in_specs = (
        P("col", "row"),
        P("col", "row"),
        P("row", "col"),
        P("row", "col"),
        P("row", "col"),
        P("row", "col"),
        P("col", "row"),
    )
    out_specs = (P("col", "row"), P("row", "col"), P("row", "col"), P("col", "row"))
    return jax.shard_map(body, mesh=mesh, in_specs=in_specs, out_specs=out_specs, check_vma=False)
```

profile of v0, /device:TPU:0, one launch (start us, length us, event | category | flops | bytes accessed | tf_op | source)
XLA Modules:
  0.0 347.5 jit_solution(18138531377756682958)
XLA Ops:
  7.2 0.0 copy-start
  7.2 0.0 all-gather.6.cloned.1.call-start
  7.2 0.7 all-gather.6.cloned.1.call-update
  7.9 0.0 reduce-scatter.3.cloned.1.call-start
  8.0 27.8 %all-gather.6.cloned.1.call-done = bf16[1024,512]{1,0:T(8,128)(2,1)} async-done(((bf16[128,512]{1,0:T(8,128)(2,1)}), bf16[1024,512]{1,0:T(8,128)(2,1)}) %all-gather.6.cloned.1.call-update) | async-done | bytes 1048592 | tf_op jit(solution)/shard_map/all_gather | solution.py:15
  35.8 0.0 copy-done
  35.8 6.3 %fusion.10 = f32[1024,1792]{1,0:T(8,128)} fusion(bf16[1024,512]{1,0:T(8,128)(2,1)} %all-gather.6.cloned.1.call-done, bf16[1792,512]{1,0:T(8,128)(2,1)S(1)} %copy-done), kind=kOutput, calls=%fused_computation.19 | convolution fusion | flops 1879048192 | bytes 10223616 | tf_op jit(solution)/shard_map/dot_general | solution.py:17
  42.1 0.0 copy-start.1
  42.1 0.0 copy-start.2
  42.1 0.0 reduce-scatter.3.cloned.1.call-update
  42.1 0.0 all-gather.8.cloned.1.call-start
  42.2 82.8 %reduce-scatter.3.cloned.1.call-done = f32[64,1792]{1,0:T(8,128)} async-done(((f32[1024,1792]{1,0:T(8,128)}), f32[64,1792]{1,0:T(8,128)}) %reduce-scatter.3.cloned.1.call-update) | async-done | bytes 458768 | tf_op jit(solution)/shard_map/reduce_scatter | solution.py:20
  124.9 0.0 copy-done.1
  124.9 0.0 copy-done.2
  124.9 2.1 fusion.9
  127.0 0.0 all-gather.8.cloned.1.call-update
  127.0 0.0 all-gather.10.cloned.1.call-start
  127.1 0.5 all-gather.10.cloned.1.call-update
  127.6 0.0 all-gather.12.cloned.1.call-start
  127.7 0.5 all-gather.12.cloned.1.call-update
  128.2 0.0 all-gather.14.cloned.1.call-start
  128.2 0.5 all-gather.14.cloned.1.call-update
  128.8 0.0 reduce-scatter.5.cloned.1.call-start
  128.8 47.9 %all-gather.8.cloned.1.call-done = bf16[1024,1792]{1,0:T(8,128)(2,1)} async-done(((bf16[64,1792]{1,0:T(8,128)(2,1)}), bf16[1024,1792]{1,0:T(8,128)(2,1)}) %all-gather.8.cloned.1.call-update) | async-done | bytes 3670032 | tf_op jit(solution)/shard_map/all_gather | solution.py:29
  176.7 6.0 %fusion.11 = f32[1024,512]{1,0:T(8,128)} fusion(bf16[1024,1792]{1,0:T(8,128)(2,1)} %all-gather.8.cloned.1.call-done, bf16[512,1792]{1,0:T(8,128)(2,1)} %param.11), kind=kOutput, calls=%fused_computation.20 | convolution fusion | flops 1879048192 | bytes 7602176 | tf_op jit(solution)/shard_map/dot_general | solution.py:31
  182.8 45.6 %all-gather.10.cloned.1.call-done = bf16[1024,1792]{1,0:T(8,128)(2,1)} async-done(((bf16[64,1792]{1,0:T(8,128)(2,1)}), bf16[1024,1792]{1,0:T(8,128)(2,1)}) %all-gather.10.cloned.1.call-update) | async-done | bytes 3670032 | tf_op jit(solution)/shard_map/all_gather | solution.py:30
  228.3 6.7 %convolution_add_fusion = f32[1024,512]{1,0:T(8,128)} fusion(f32[1024,512]{1,0:T(8,128)} %fusion.11, bf16[1024,1792]{1,0:T(8,128)(2,1)} %all-gather.10.cloned.1.call-done, bf16[512,1792]{1,0:T(8,128)(2,1)} %param.12), kind=kOutput, calls=%fused_computation.2 | convolution fusion | flops 1879572480 | bytes 9699328 | tf_op jit(solution)/shard_map/dot_general | solution.py:33
  235.1 0.0 reduce-scatter.5.cloned.1.call-update
  235.1 17.7 %all-gather.12.cloned.1.call-done = bf16[1024,512]{1,0:T(8,128)(2,1)} async-done(((bf16[128,512]{1,0:T(8,128)(2,1)}), bf16[1024,512]{1,0:T(8,128)(2,1)}) %all-gather.12.cloned.1.call-update) | async-done | bytes 1048592 | tf_op jit(solution)/shard_map/all_gather | solution.py:21
  252.8 6.3 %convolution_bitcast_fusion.1 = f32[512,1792]{0,1:T(8,128)} fusion(bf16[1024,1792]{1,0:T(8,128)(2,1)} %all-gather.8.cloned.1.call-done, bf16[1024,512]{1,0:T(8,128)(2,1)} %all-gather.12.cloned.1.call-done), kind=kOutput, calls=%fused_computation.1 | convolution fusion | flops 1879048192 | bytes 8388608 | tf_op jit(solution)/shard_map/dot_general | solution.py:38
  259.1 0.0 copy-start.4
  259.1 5.2 %copy.11 = f32[512,1792]{1,0:T(8,128)} copy(f32[512,1792]{0,1:T(8,128)} %convolution_bitcast_fusion.1) | data formatting | bytes 7340032
  264.3 0.0 copy-done.4
  264.3 6.1 %convolution_bitcast_fusion = f32[512,1792]{0,1:T(8,128)} fusion(bf16[1024,1792]{1,0:T(8,128)(2,1)} %all-gather.10.cloned.1.call-done, bf16[1024,512]{1,0:T(8,128)(2,1)S(1)} %copy-done.4), kind=kOutput, calls=%fused_computation | convolution fusion | flops 1879048192 | bytes 8388608 | tf_op jit(solution)/shard_map/dot_general | solution.py:39
  270.4 0.0 copy-start.3
  270.4 5.2 %copy.12 = f32[512,1792]{1,0:T(8,128)} copy(f32[512,1792]{0,1:T(8,128)} %convolution_bitcast_fusion) | data formatting | bytes 7340032
  275.7 28.9 %all-gather.14.cloned.1.call-done = bf16[1024,1792]{1,0:T(8,128)(2,1)} async-done(((bf16[64,1792]{1,0:T(8,128)(2,1)}), bf16[1024,1792]{1,0:T(8,128)(2,1)}) %all-gather.14.cloned.1.call-update) | async-done | bytes 3670032 | tf_op jit(solution)/shard_map/all_gather | solution.py:16
  304.5 0.0 copy-done.3
  304.5 6.0 %fusion.12 = f32[1792,512]{1,0:T(8,128)} fusion(bf16[1024,1792]{1,0:T(8,128)(2,1)} %all-gather.14.cloned.1.call-done, bf16[1024,512]{1,0:T(8,128)(2,1)S(1)} %copy-done.3), kind=kOutput, calls=%fused_computation.21 | convolution fusion | flops 1879048192 | bytes 8388608 | tf_op jit(solution)/shard_map/dot_general | solution.py:26
  310.5 30.2 %reduce-scatter.5.cloned.1.call-done = f32[128,512]{1,0:T(8,128)} async-done(((f32[1024,512]{1,0:T(8,128)}), f32[128,512]{1,0:T(8,128)}) %reduce-scatter.5.cloned.1.call-update) | async-done | bytes 262160 | tf_op jit(solution)/shard_map/reduce_scatter | solution.py:32
Async XLA Ops:
  7.2 28.6 %copy-start = (bf16[1792,512]{1,0:T(8,128)(2,1)S(1)}, bf16[1792,512]{1,0:T(8,128)(2,1)}, u32[]{:S(2)}) copy-start(bf16[1792,512]{1,0:T(8,128)(2,1)} %param.13) | copy-start | bytes 5505028
  7.2 28.6 %all-gather.6.cloned.1.call-start = ((), (), s32[]{:S(2)}) async-start(), calls=%async_computation.2 | async-start | bytes 1179648 | tf_op jit(solution)/shard_map/all_gather | solution.py:15
  7.9 117.0 %reduce-scatter.3.cloned.1.call-start = ((), (), s32[]{:S(2)}) async-start(), calls=%async_computation.3 | async-start | bytes 7798784 | tf_op jit(solution)/shard_map/reduce_scatter | solution.py:20
  42.1 82.8 %copy-start.1 = (bf16[64,1792]{1,0:T(8,128)(2,1)S(1)}, bf16[64,1792]{1,0:T(8,128)(2,1)}, u32[]{:S(2)}) copy-start(bf16[64,1792]{1,0:T(8,128)(2,1)} %param.9) | copy-start | bytes 688132
  42.1 82.8 %copy-start.2 = (bf16[64,1792]{1,0:T(8,128)(2,1)S(1)}, bf16[64,1792]{1,0:T(8,128)(2,1)}, u32[]{:S(2)}) copy-start(bf16[64,1792]{1,0:T(8,128)(2,1)} %param.10) | copy-start | bytes 688132
  42.1 134.6 %all-gather.8.cloned.1.call-start = ((), (), s32[]{:S(2)}) async-start(), calls=%async_computation.4 | async-start | bytes 3899392 | tf_op jit(solution)/shard_map/all_gather | solution.py:29
  127.0 101.3 %all-gather.10.cloned.1.call-start = ((), (), s32[]{:S(2)}) async-start(), calls=%async_computation.5 | async-start | bytes 3899392 | tf_op jit(solution)/shard_map/all_gather | solution.py:30
  127.6 125.2 %all-gather.12.cloned.1.call-start = ((), (), s32[]{:S(2)}) async-start(), calls=%async_computation.7 | async-start | bytes 1179648 | tf_op jit(solution)/shard_map/all_gather | solution.py:21
  128.2 176.3 %all-gather.14.cloned.1.call-start = ((), (), s32[]{:S(2)}) async-start(), calls=%async_computation.8 | async-start | bytes 3899392 | tf_op jit(solution)/shard_map/all_gather | solution.py:16
  128.8 211.9 %reduce-scatter.5.cloned.1.call-start = ((), (), s32[]{:S(2)}) async-start(), calls=%async_computation.6 | async-start | bytes 2359296 | tf_op jit(solution)/shard_map/reduce_scatter | solution.py:32
  259.1 5.2 %copy-start.4 = (bf16[1024,512]{1,0:T(8,128)(2,1)S(1)}, bf16[1024,512]{1,0:T(8,128)(2,1)}, u32[]{:S(2)}) copy-start(bf16[1024,512]{1,0:T(8,128)(2,1)} %all-gather.12.cloned.1.call-done) | copy-start | bytes 3145732
  270.4 34.1 %copy-start.3 = (bf16[1024,512]{1,0:T(8,128)(2,1)S(1)}, bf16[1024,512]{1,0:T(8,128)(2,1)}, u32[]{:S(2)}) copy-start(bf16[1024,512]{1,0:T(8,128)(2,1)} %all-gather.6.cloned.1.call-done) | copy-start | bytes 3145732
Sparse Core Ops, SparseCore 0:
  9.7 26.0 all-gather.5
  42.2 82.6 reduce-scatter.2
  127.9 48.8 all-gather.7
  179.5 48.7 all-gather.9
  230.0 22.7 all-gather.11
  255.1 49.4 all-gather.13
  307.6 32.9 reduce-scatter.4
where the time goes:
time: 348 us; the launch traced here: 347 us
  waiting for transfers between devices  283 us (81%)
  matrix products  37.4 us (11%)
  between operations  14.1 us (4%)
  local copies, waits for them, and re-layouts  10.5 us (3%)
    reduce_scatter x1, waiting for transfers between devices, body(): lax.psum_scatter(partial_sum, 'row', scatter_dimension=0, tiled=True)  82.8 us
    all_gather x1, waiting for transfers between devices, body(): gate_all = lax.all_gather(grad_gate, 'row', axis=0, tiled=True)  47.9 us
    all_gather x1, waiting for transfers between devices, body(): up_all = lax.all_gather(grad_up, 'row', axis=0, tiled=True)  45.6 us
    reduce_scatter x1, waiting for transfers between devices, body(): lax.psum_scatter(total + lax.dot_general(up_all, up_weight, LAST_DIMS, pr...  30.2 us
    all_gather x1, waiting for transfers between devices, body(): hidden_all = lax.all_gather(hidden, 'row', axis=0, tiled=True)  28.9 us
    all_gather x1, waiting for transfers between devices, body(): grad_full = lax.all_gather(out_grad, 'col', axis=0, tiled=True)  27.8 us
    all_gather x1, waiting for transfers between devices, body(): input_full = lax.all_gather(inputs, 'col', axis=0, tiled=True)  17.7 us
    unnamed x12, local copies, waits for them, and re-layouts  10.5 us
  transfers between devices with their start and end apart: 7, of which 7 were waited for; matrix products, arithmetic and copies ran while one was open for 12% of the time, Pallas kernels for 0%

commit v1 on v0

--- a/solution.py
+++ b/solution.py
@@ -26,7 +26,9 @@
     down_grad = lax.dot_general(
         hidden_all, grad_full, LEAD_DIMS, preferred_element_type=jnp.float32
     )
-    gate_all = lax.all_gather(grad_gate, "row", axis=0, tiled=True)
+    gate_all = jnp.concatenate(
+        lax.all_to_all(jnp.stack([grad_gate] * lax.axis_size("row"), axis=0), "row", 0, 0), axis=0
+    )
     up_all = lax.all_gather(grad_up, "row", axis=0, tiled=True)
     total = lax.dot_general(gate_all, gate_weight, LAST_DIMS, preferred_element_type=jnp.float32)
     input_grad = lax.psum_scatter(

time: 348 us -> 319 us (0.917)
  waiting for transfers between devices: 283 us -> 201 us
  blocking collectives: 0 us -> 53.5 us
    all_to_all x0 -> x1, blocking collectives: none -> 53.5 us  [body(): lax.all_to_all(jnp.stack([grad_gate] * lax.axis_size('row'), axis=0), 'ro...]
    all_gather x1 -> x0, waiting for transfers between devices: 47.9 us -> none  [body(): gate_all = lax.all_gather(grad_gate, 'row', axis=0, tiled=True)]
    all_gather x1, waiting for transfers between devices: 45.6 us -> 12.2 us  [body(): up_all = lax.all_gather(grad_up, 'row', axis=0, tiled=True)]
    unnamed x12 -> x16, local copies, waits for them, and re-layouts: 10.5 us -> 12.3 us
  transfers between devices with their start and end apart: 7 -> 6, of which waited for: 7 -> 6; matrix products, arithmetic and copies ran while one was open for 12% -> 12% of each run, Pallas kernels for 0% -> 0%
where the time goes in v1:
time: 319 us
  waiting for transfers between devices  201 us (63%)
  blocking collectives  53.5 us (17%)
  matrix products  34.8 us (11%)
  between operations  14.1 us (4%)
  local copies, waits for them, and re-layouts  12.7 us (4%)
    reduce_scatter x1, waiting for transfers between devices, body(): lax.psum_scatter(partial_sum, 'row', scatter_dimension=0, tiled=True)  82.8 us
    all_to_all x1, blocking collectives, body(): lax.all_to_all(jnp.stack([grad_gate] * lax.axis_size('row'), axis=0), 'ro...  53.5 us
    reduce_scatter x1, waiting for transfers between devices, body(): lax.psum_scatter(total + lax.dot_general(up_all, up_weight, LAST_DIMS, pr...  30 us
    all_gather x1, waiting for transfers between devices, body(): hidden_all = lax.all_gather(hidden, 'row', axis=0, tiled=True)  28.9 us
    all_gather x1, waiting for transfers between devices, body(): grad_full = lax.all_gather(out_grad, 'col', axis=0, tiled=True)  27.8 us
    all_gather x1, waiting for transfers between devices, body(): input_full = lax.all_gather(inputs, 'col', axis=0, tiled=True)  17.8 us
    unnamed x16, local copies, waits for them, and re-layouts  12.3 us
    all_gather x1, waiting for transfers between devices, body(): up_all = lax.all_gather(grad_up, 'row', axis=0, tiled=True)  12.2 us
  transfers between devices with their start and end apart: 6, of which 6 were waited for; matrix products, arithmetic and copies ran while one was open for 12% of the time, Pallas kernels for 0%

profile of v1, /device:TPU:0, one launch (start us, length us, event | category | flops | bytes accessed | tf_op | source)
XLA Modules:
  0.0 318.6 jit_solution(1621211691455223189)
XLA Ops:
  7.2 0.0 copy-start
  7.2 0.0 all-gather.5.cloned.1.call-start
  7.2 0.7 all-gather.5.cloned.1.call-update
  7.9 0.0 reduce-scatter.3.cloned.1.call-start
  8.0 27.8 %all-gather.5.cloned.1.call-done = bf16[1024,512]{1,0:T(8,128)(2,1)} async-done(((bf16[128,512]{1,0:T(8,128)(2,1)}), bf16[1024,512]{1,0:T(8,128)(2,1)}) %all-gather.5.cloned.1.call-update) | async-done | bytes 1048592 | tf_op jit(solution)/shard_map/all_gather | solution.py:15
  35.8 0.0 copy-done
  35.8 6.3 %fusion.10 = f32[1024,1792]{1,0:T(8,128)} fusion(bf16[1024,512]{1,0:T(8,128)(2,1)} %all-gather.5.cloned.1.call-done, bf16[1792,512]{1,0:T(8,128)(2,1)S(1)} %copy-done), kind=kOutput, calls=%fused_computation.19 | convolution fusion | flops 1879048192 | bytes 10223616 | tf_op jit(solution)/shard_map/dot_general | solution.py:17
  42.1 0.0 copy-start.2
  42.1 0.0 copy-start.3
  42.1 0.0 reduce-scatter.3.cloned.1.call-update
  42.1 0.0 all-gather.7.cloned.1.call-start
  42.2 82.8 %reduce-scatter.3.cloned.1.call-done = f32[64,1792]{1,0:T(8,128)} async-done(((f32[1024,1792]{1,0:T(8,128)}), f32[64,1792]{1,0:T(8,128)}) %reduce-scatter.3.cloned.1.call-update) | async-done | bytes 458768 | tf_op jit(solution)/shard_map/reduce_scatter | solution.py:20
  124.9 0.0 copy-done.2
  124.9 0.0 copy-done.3
  124.9 2.1 fusion.9
  127.0 0.0 all-gather.7.cloned.1.call-update
  127.0 0.0 all-gather.9.cloned.1.call-start
  127.1 0.5 all-gather.9.cloned.1.call-update
  127.6 0.0 all-gather.11.cloned.1.call-start
  127.6 0.5 all-gather.11.cloned.1.call-update
  128.2 0.0 reduce-scatter.5.cloned.1.call-start
  128.2 0.4 stack.2
  128.6 0.0 copy-start.4
  128.6 53.5 %all_to_all.5 = bf16[16,64,1792]{2,1,0:T(8,128)(2,1)S(1)} all-to-all(bf16[16,64,1792]{2,1,0:T(8,128)(2,1)S(1)} %stack.2), channel_id=1, replica_groups=mesh['row'=16,'col'=8] {'row'}, dimensions={0} | all-to-all | bytes 7340032 | tf_op jit(solution)/shard_map/all_to_all | solution.py:30
  182.1 0.0 copy-start.1
  182.1 1.8 copy-done.1
  183.9 0.0 copy-done.4
  183.9 3.4 %fusion.11 = f32[1024,512]{1,0:T(8,128)} fusion(bf16[1024,1792]{1,0:T(8,128)(2,1)S(1)} %bitcast.17, bf16[512,1792]{1,0:T(8,128)(2,1)S(1)} %copy-done.4), kind=kOutput, calls=%fused_computation.20 | convolution fusion | flops 1879048192 | bytes 7602176 | tf_op jit(solution)/shard_map/dot_general | solution.py:33
  187.3 12.2 %all-gather.7.cloned.1.call-done = bf16[1024,1792]{1,0:T(8,128)(2,1)} async-done(((bf16[64,1792]{1,0:T(8,128)(2,1)}), bf16[1024,1792]{1,0:T(8,128)(2,1)}) %all-gather.7.cloned.1.call-update) | async-done | bytes 3670032 | tf_op jit(solution)/shard_map/all_gather | solution.py:32
  199.5 6.7 %convolution_add_fusion = f32[1024,512]{1,0:T(8,128)} fusion(f32[1024,512]{1,0:T(8,128)} %fusion.11, bf16[1024,1792]{1,0:T(8,128)(2,1)} %all-gather.7.cloned.1.call-done, bf16[512,1792]{1,0:T(8,128)(2,1)} %param.12), kind=kOutput, calls=%fused_computation.2 | convolution fusion | flops 1879572480 | bytes 9699328 | tf_op jit(solution)/shard_map/dot_general | solution.py:35
  206.3 0.0 reduce-scatter.5.cloned.1.call-update
  206.3 17.8 %all-gather.9.cloned.1.call-done = bf16[1024,512]{1,0:T(8,128)(2,1)} async-done(((bf16[128,512]{1,0:T(8,128)(2,1)}), bf16[1024,512]{1,0:T(8,128)(2,1)}) %all-gather.9.cloned.1.call-update) | async-done | bytes 1048592 | tf_op jit(solution)/shard_map/all_gather | solution.py:21
  224.1 6.3 %convolution_bitcast_fusion.1 = f32[512,1792]{0,1:T(8,128)} fusion(bf16[1024,1792]{1,0:T(8,128)(2,1)} %bitcast.18, bf16[1024,512]{1,0:T(8,128)(2,1)} %all-gather.9.cloned.1.call-done), kind=kOutput, calls=%fused_computation.1 | convolution fusion | flops 1879048192 | bytes 8388608 | tf_op jit(solution)/shard_map/dot_general | solution.py:40
  230.3 0.0 copy-start.6
  230.3 5.2 %copy.11 = f32[512,1792]{1,0:T(8,128)} copy(f32[512,1792]{0,1:T(8,128)} %convolution_bitcast_fusion.1) | data formatting | bytes 7340032
  235.5 0.0 copy-done.6
  235.5 6.1 %convolution_bitcast_fusion = f32[512,1792]{0,1:T(8,128)} fusion(bf16[1024,1792]{1,0:T(8,128)(2,1)} %all-gather.7.cloned.1.call-done, bf16[1024,512]{1,0:T(8,128)(2,1)S(1)} %copy-done.6), kind=kOutput, calls=%fused_computation | convolution fusion | flops 1879048192 | bytes 8388608 | tf_op jit(solution)/shard_map/dot_general | solution.py:41
  241.6 0.0 copy-start.5
  241.6 5.2 %copy.12 = f32[512,1792]{1,0:T(8,128)} copy(f32[512,1792]{0,1:T(8,128)} %convolution_bitcast_fusion) | data formatting | bytes 7340032
  246.9 28.9 %all-gather.11.cloned.1.call-done = bf16[1024,1792]{1,0:T(8,128)(2,1)} async-done(((bf16[64,1792]{1,0:T(8,128)(2,1)}), bf16[1024,1792]{1,0:T(8,128)(2,1)}) %all-gather.11.cloned.1.call-update) | async-done | bytes 3670032 | tf_op jit(solution)/shard_map/all_gather | solution.py:16
  275.7 0.0 copy-done.5
  275.7 6.0 %fusion.12 = f32[1792,512]{1,0:T(8,128)} fusion(bf16[1024,1792]{1,0:T(8,128)(2,1)} %all-gather.11.cloned.1.call-done, bf16[1024,512]{1,0:T(8,128)(2,1)S(1)} %copy-done.5), kind=kOutput, calls=%fused_computation.21 | convolution fusion | flops 1879048192 | bytes 8388608 | tf_op jit(solution)/shard_map/dot_general | solution.py:26
  281.7 30.0 %reduce-scatter.5.cloned.1.call-done = f32[128,512]{1,0:T(8,128)} async-done(((f32[1024,512]{1,0:T(8,128)}), f32[128,512]{1,0:T(8,128)}) %reduce-scatter.5.cloned.1.call-update) | async-done | bytes 262160 | tf_op jit(solution)/shard_map/reduce_scatter | solution.py:34
Async XLA Ops:
  7.2 28.6 %copy-start = (bf16[1792,512]{1,0:T(8,128)(2,1)S(1)}, bf16[1792,512]{1,0:T(8,128)(2,1)}, u32[]{:S(2)}) copy-start(bf16[1792,512]{1,0:T(8,128)(2,1)} %param.13) | copy-start | bytes 5505028
  7.2 28.6 %all-gather.5.cloned.1.call-start = ((), (), s32[]{:S(2)}) async-start(), calls=%async_computation.3 | async-start | bytes 1179648 | tf_op jit(solution)/shard_map/all_gather | solution.py:15
  7.9 117.0 %reduce-scatter.3.cloned.1.call-start = ((), (), s32[]{:S(2)}) async-start(), calls=%async_computation.4 | async-start | bytes 7798784 | tf_op jit(solution)/shard_map/reduce_scatter | solution.py:20
  42.1 82.8 %copy-start.2 = (bf16[64,1792]{1,0:T(8,128)(2,1)S(1)}, bf16[64,1792]{1,0:T(8,128)(2,1)}, u32[]{:S(2)}) copy-start(bf16[64,1792]{1,0:T(8,128)(2,1)} %param.9) | copy-start | bytes 688132
  42.1 82.8 %copy-start.3 = (bf16[64,1792]{1,0:T(8,128)(2,1)S(1)}, bf16[64,1792]{1,0:T(8,128)(2,1)}, u32[]{:S(2)}) copy-start(bf16[64,1792]{1,0:T(8,128)(2,1)} %param.10) | copy-start | bytes 688132
  42.1 157.4 %all-gather.7.cloned.1.call-start = ((), (), s32[]{:S(2)}) async-start(), calls=%async_computation.5 | async-start | bytes 3899392 | tf_op jit(solution)/shard_map/all_gather | solution.py:32
  127.0 97.0 %all-gather.9.cloned.1.call-start = ((), (), s32[]{:S(2)}) async-start(), calls=%async_computation.7 | async-start | bytes 1179648 | tf_op jit(solution)/shard_map/all_gather | solution.py:21
  127.6 148.1 %all-gather.11.cloned.1.call-start = ((), (), s32[]{:S(2)}) async-start(), calls=%async_computation.8 | async-start | bytes 3899392 | tf_op jit(solution)/shard_map/all_gather | solution.py:16
  128.2 183.5 %reduce-scatter.5.cloned.1.call-start = ((), (), s32[]{:S(2)}) async-start(), calls=%async_computation.6 | async-start | bytes 2359296 | tf_op jit(solution)/shard_map/reduce_scatter | solution.py:34
  128.6 55.3 %copy-start.4 = (bf16[512,1792]{1,0:T(8,128)(2,1)S(1)}, bf16[512,1792]{1,0:T(8,128)(2,1)}, u32[]{:S(2)}) copy-start(bf16[512,1792]{1,0:T(8,128)(2,1)} %param.11) | copy-start | bytes 5505028
  182.1 1.8 copy-start.1
  230.3 5.2 %copy-start.6 = (bf16[1024,512]{1,0:T(8,128)(2,1)S(1)}, bf16[1024,512]{1,0:T(8,128)(2,1)}, u32[]{:S(2)}) copy-start(bf16[1024,512]{1,0:T(8,128)(2,1)} %all-gather.9.cloned.1.call-done) | copy-start | bytes 3145732
  241.6 34.1 %copy-start.5 = (bf16[1024,512]{1,0:T(8,128)(2,1)S(1)}, bf16[1024,512]{1,0:T(8,128)(2,1)}, u32[]{:S(2)}) copy-start(bf16[1024,512]{1,0:T(8,128)(2,1)} %all-gather.5.cloned.1.call-done) | copy-start | bytes 3145732
Sparse Core Ops, SparseCore 0:
  9.7 26.0 all-gather.4
  42.2 82.6 reduce-scatter.2
  127.9 71.6 all-gather.6
  201.2 22.7 all-gather.8
  226.3 49.4 all-gather.10
  278.7 32.9 reduce-scatter.4
